TPU v7x, 32 devices: a whole 2x2x4 slice. The times are simulated.
32 devices in a mesh: inp: 4 (over y, x), chan: 8 (over z, core).
Axes of the slice: x: 2, y: 2, z: 4, core: 2. Of those that a mesh axis runs over, the one named last changes fastest.
Arguments:
- voltages: bfloat16 [128, 128, 8192], P('inp', 'chan'), may hold values from -6 to 6
- history: bfloat16 [128, 7, 8192], P('inp'), may hold values from -6 to 6
- taper: float32 [8, 8192], replicated, may hold values from -2 to 2
Outputs:
- visibility: bfloat16 [2, 2048, 128, 128], P(None, ('inp', 'chan'))
All inputs are finite; a program needn't handle non-finite values.
Results may differ from a plain program's by a relative error of at most 0.005.
Values may be sent and summed in bfloat16 or wider, within the bound.
No kernel may reach another device: no remote copies, remote signals or barrier semaphores. Data moves between devices by JAX's collectives and lax.ppermute only.
A program may use at most 192 MiB of HBM per device.

v0:
```python
import math

import jax
import jax.numpy as jnp
import ml_dtypes
import numpy as np
from jax import lax
from jax.experimental import pallas as pl
from jax.experimental.pallas import tpu as pltpu
from jax.sharding import PartitionSpec as P

BAND = 2048
LOW = 1024
LANES = 128
RADIX = 64
HALF = 16
PAIR = 2
BLOCK = 16
CLASSES = RADIX // 2
ROOT = math.sqrt(0.5)
F32 = jnp.float32
BF16 = jnp.bfloat16
VMEM = 63 * 1024 * 1024


def stage_table(frame):
    high = BAND // RADIX
    lane = np.arange(LANES)
    table = np.zeros((CLASSES, 2, high, 2, 2, LANES))
    for q in range(CLASSES):
        for half in range(2):
            low = q if half == 0 else (RADIX - q if q else RADIX // 2)
            k = low + RADIX * (LOW // RADIX + np.arange(high))
            angle = 2.0 * np.pi * (np.outer(k, lane) % frame) / frame
            cos, sin = np.cos(angle), np.sin(angle)
            if q == 0:
                table[q, half, :, 0, half] = cos
                table[q, half, :, 1, half] = -sin
            elif half == 0:
                table[q, half, :, 0, 0] = cos
                table[q, half, :, 0, 1] = sin
                table[q, half, :, 1, 0] = -sin
                table[q, half, :, 1, 1] = cos
            else:
                table[q, half, :, 0, 0] = cos
                table[q, half, :, 0, 1] = -sin
                table[q, half, :, 1, 0] = -sin
                table[q, half, :, 1, 1] = -cos
    table = table / math.sqrt(frame)
    return table.swapaxes(2, 3).reshape(CLASSES, 2 * high * 2, 2 * LANES)


def real_dft8(x):
    s = [x[j] + x[j + 4] for j in range(4)]
    d = [x[j] - x[j + 4] for j in range(4)]
    e0, e1 = s[0] + s[2], s[0] - s[2]
    o0, o1 = s[1] + s[3], s[3] - s[1]
    u, v = (d[1] - d[3]) * ROOT, (d[1] + d[3]) * ROOT
    return [
        (e0 + o0, None),
        (d[0] + u, -(d[2] + v)),
        (e1, o1),
        (d[0] - u, d[2] - v),
        (e0 - o0, None),
    ]


def complex_dft8(x):
    def add(a, b):
        return (a[0] + b[0], a[1] + b[1])

    def sub(a, b):
        return (a[0] - b[0], a[1] - b[1])

    def add_i(a, b):
        return (a[0] - b[1], a[1] + b[0])

    def sub_i(a, b):
        return (a[0] + b[1], a[1] - b[0])

    s = [add(x[j], x[j + 4]) for j in range(4)]
    d = [sub(x[j], x[j + 4]) for j in range(4)]
    e0, e1 = add(s[0], s[2]), sub(s[0], s[2])
    o0, o1 = add(s[1], s[3]), sub(s[1], s[3])
    p, m = sub(d[1], d[3]), add(d[1], d[3])
    b = ((p[0] + m[1]) * ROOT, (p[1] - m[0]) * ROOT)
    c = ((m[1] - p[0]) * ROOT, (-p[1] - m[0]) * ROOT)
    f, g = sub_i(d[0], d[2]), add_i(d[0], d[2])
    return [
        add(e0, o0),
        add(f, b),
        sub_i(e1, o1),
        add(g, c),
        sub(e0, o0),
        sub(f, b),
        add_i(e1, o1),
        sub(g, c),
    ]


def turned(value, step):
    angle = 2.0 * math.pi * (step % RADIX) / RADIX
    cos, sin = math.cos(angle), math.sin(angle)
    real, imag = value
    if imag is None:
        return (real * cos, real * -sin)
    if step % RADIX == 0:
        return value
    return (real * cos + imag * sin, imag * cos - real * sin)


def unrolled(count, copies, body):
    def step(i, carry):
        for copy in range(copies):
            body(i * copies + copy, copy)
        return carry

    lax.fori_loop(0, count // copies, step, 0)


def transform_rows(fir, mids, zed, half, copies):
    halves = zed.shape[1] // (fir.shape[1] * HALF)

    def one(s, copy):
        mid = mids.at[copy]
        for low in range(8):
            parts = real_dft8([fir[8 * high + low, s] for high in range(8)])
            mid[0, low] = parts[0][0]
            mid[7, low] = parts[4][0]
            for k in (1, 2, 3):
                value = turned(parts[k], low * k)
                mid[2 * k - 1, low] = value[0]
                mid[2 * k, low] = value[1]
        rows = pl.ds(pl.multiple_of((s * halves + half) * HALF, HALF), HALF)

        def put(q, half, value):
            zed[q, rows, half * LANES : (half + 1) * LANES] = value.astype(BF16)

        parts = real_dft8([mid[0, low] for low in range(8)])
        put(0, 0, parts[0][0])
        put(0, 1, parts[4][0])
        for m in (1, 2, 3):
            put(8 * m, 0, parts[m][0])
            put(8 * m, 1, parts[m][1])
        for k in (1, 2, 3):
            parts = complex_dft8([(mid[2 * k - 1, low], mid[2 * k, low]) for low in range(8)])
            for m in range(8):
                index = k + 8 * m
                if index < CLASSES:
                    put(index, 0, parts[m][0])
                    put(index, 1, parts[m][1])
                else:
                    put(RADIX - index, 0, parts[m][0])
                    put(RADIX - index, 1, -parts[m][1])
        parts = complex_dft8([turned((mid[7, low], None), 4 * low) for low in range(8)])
        for m in range(4):
            put(4 + 8 * m, 0, parts[m][0])
            put(4 + 8 * m, 1, parts[m][1])

    unrolled(fir.shape[1], copies, one)


CHUNKS = 4
CONTRACT = (((1,), (1,)), ((), ()))


def fill(first, copies, hist, keep, volt_in, taper_in, table_in, volt, taper, held, fir, mid, zed, sems):
    taps = taper.shape[0]
    in_dev, s_dev, frame = volt.shape
    halves = in_dev // HALF
    count = fir.shape[1]
    part = frame // CHUNKS
    wanted = [f for f in range(first - taps + 1, first + count) if f < s_dev]

    def volt_copy(h, j):
        where = (pl.ds(h * HALF, HALF), slice(None), pl.ds(pl.multiple_of(j * part, part), part))
        return pltpu.make_async_copy(volt_in.at[where], volt.at[where], sems.at[h * CHUNKS + j])

    taper_copy = pltpu.make_async_copy(taper_in, taper, sems.at[halves * CHUNKS])
    table_copy = pltpu.make_async_copy(table_in, held, sems.at[halves * CHUNKS + 1])
    taper_copy.start()
    for h in range(halves):
        for j in range(CHUNKS):
            volt_copy(h, j).start()
    table_copy.start()
    taper_copy.wait()

    def one_half(h, carry):
        inputs = pl.ds(pl.multiple_of(h * HALF, HALF), HALF)

        def one_chunk(j, carry):
            volt_copy(h, j).wait()

            def one(i, copy):
                a = j * (part // LANES) + i
                lanes = pl.ds(pl.multiple_of(a * LANES, LANES), LANES)
                by_time = jnp.swapaxes(volt[inputs, :, lanes], 0, 1)
                frames = {}
                for f in wanted:
                    if f >= 0:
                        frames[f] = by_time[f].astype(F32)
                    elif hist is not None:
                        frames[f] = hist[taps - 1 + f, inputs, lanes].astype(F32) * keep
                weights = [taper[t : t + 1, lanes] for t in range(taps)]
                for row in range(count):
                    total = None
                    for t in range(taps):
                        f = first + row + t - taps + 1
                        if f in frames:
                            term = weights[t] * frames[f]
                            total = term if total is None else total + term
                    fir[a, row] = total

            unrolled(part // LANES, copies[0], one)
            return carry

        lax.fori_loop(0, CHUNKS, one_chunk, 0)
        transform_rows(fir, mid, zed, h, copies[1])
        return carry

    lax.fori_loop(0, halves, one_half, 0)
    table_copy.wait()


def carried_kernel(volt_in, taper_in, table_in, out_ref, *scratch):
    *scratch, out, out_sems = scratch
    volt, taper, held, fir, mid, zed, sems = scratch
    fill(
        volt.shape[1], (16, 1), None, None,
        volt_in, taper_in, table_in, volt, taper, held, fir, mid, zed, sems,
    )
    block = CLASSES // 2

    def out_copy(j):
        where = pl.ds(j * block, block)
        return pltpu.make_async_copy(out.at[where], out_ref.at[where], out_sems.at[j])

    def some(j, carry):
        for i in range(block):
            q = j * block + i
            out[q] = jnp.dot(zed[q], held[q], preferred_element_type=F32).astype(BF16)
        out_copy(j).start()
        return carry

    lax.fori_loop(0, 2, some, 0)

    def finish(j, carry):
        out_copy(j).wait()
        return carry

    lax.fori_loop(0, 2, finish, 0)


def lane_swap(x):
    width = LANES // 4
    block = lax.broadcasted_iota(jnp.int32, (HALF, LANES), 1) // width
    x = list(x)
    mask = (block & 1) == 0
    for p in (0, 2):
        low, up = x[p], x[p + 1]
        x[p] = jnp.where(mask, low, pltpu.roll(up, width, 1))
        x[p + 1] = jnp.where(mask, pltpu.roll(low, LANES - width, 1), up)
    mask = (block & 2) == 0
    for p in (0, 1):
        low, up = x[p], x[p + 2]
        moved = pltpu.roll(jnp.where(mask, up, low), 2 * width, 1)
        x[p] = jnp.where(mask, low, moved)
        x[p + 2] = jnp.where(mask, moved, up)
    return x


def spectra_kernel(first, boundary, *refs):
    if boundary:
        keep, hist, carried, unit, *refs = refs
        keep = keep[0]
    else:
        keep, hist = None, None
    volt_in, taper_in, table_in, out_ref, volt, taper, held, fir, mid, zed, sems, wide, out = refs
    fill(
        first, (16, 4) if boundary else (8, 2), hist, keep,
        volt_in, taper_in, table_in, volt, taper, held, fir, mid, zed, sems,
    )
    step = RADIX
    high = step // 2
    sides = wide.shape[2] // LANES
    split = out.shape[0] // high
    channels = RADIX // split

    def one(q, copy):
        value = lax.dot_general(held[q], zed[q], CONTRACT, preferred_element_type=F32)
        if boundary:
            part = carried[q]
            short = zed.shape[1] - part.shape[0]
            part = jnp.concatenate([part, jnp.zeros((short, LANES), BF16)], axis=0)
            value = value + lax.dot_general(
                unit[...], part, CONTRACT, preferred_element_type=F32
            )
        wide[q] = value[:step].astype(BF16)
        wide[jnp.where(q == 0, CLASSES, RADIX - q)] = value[step:].astype(BF16)

    unrolled(CLASSES, 4 if boundary else 16, one)

    def out_copy(b):
        where = pl.ds(b * HALF * split, HALF * split)
        return pltpu.make_async_copy(out.at[where], out_ref.at[where], sems.at[b])

    def rows_of(b, part):
        return pl.ds(pl.multiple_of(part * high + b * HALF, HALF), HALF)

    def late_block(b, copy):
        for part in range(2):
            for side in range(sides):
                lanes = slice(side * LANES, (side + 1) * LANES)
                for first_k in range(0, RADIX, HALF):
                    value = jnp.swapaxes(
                        wide[first_k : first_k + HALF, rows_of(b, part), lanes], 0, 1
                    )
                    u, k = divmod(first_k, channels)
                    start = part * channels + k
                    for j in range(HALF):
                        group = (b * HALF + j) * split + u
                        out[group, side, start : start + HALF, :] = value[j]
        out_copy(b).start()

    def early_block(b, copy):
        def quad(k, copy):
            tiles = []
            for part in range(2):
                for side in range(sides):
                    lanes = slice(side * LANES, (side + 1) * LANES)
                    tiles += lane_swap([wide[4 * k + p, rows_of(b, part), lanes] for p in range(4)])
            value = jnp.swapaxes(jnp.stack(tiles), 0, 1)
            u, inside = lax.div(k, channels // 4), lax.rem(k, channels // 4)
            for j in range(HALF):
                out[(b * HALF + j) * split + u, inside] = value[j]

        unrolled(RADIX // 4, 4, quad)
        out_copy(b).start()

    unrolled(high // HALF, 1, early_block if boundary else late_block)

    def finish(b, carry):
        out_copy(b).wait()
        return carry

    lax.fori_loop(0, high // HALF, finish, 0)


def reorder(got, first, copies, put):
    n_inp, _, sets, rows, _ = got.shape
    assert HALF // (sets * PAIR) == 4

    def one(b, copy):
        here = pl.ds(pl.multiple_of(b * HALF, HALF), HALF)
        for tile in range(n_inp // 4):
            pieces = []
            for c in range(PAIR):
                for part in range(sets):
                    pieces += lane_swap(
                        [got[tile * 4 + p, first + c, part, here, :] for p in range(4)]
                    )
            value = jnp.swapaxes(jnp.stack(pieces), 0, 1)
            for j in range(HALF):
                put(b * HALF + j, tile, value[j])

    unrolled(rows // HALF, min(copies, rows // HALF), one)


def order_pair(got, j, copies, out):
    def put(r, tile, value):
        times = pl.ds(pl.multiple_of(j * HALF, HALF), HALF)
        out[r, times, tile * LANES : (tile + 1) * LANES] = value

    reorder(got, j * PAIR, copies, put)


def gram(left, right):
    return lax.dot_general(
        left,
        jnp.concatenate([left, right], axis=1),
        (((0,), (0,)), ((), ())),
        preferred_element_type=F32,
    )


def prior_kernel(got, out, rows):
    channels = out.shape[0]

    def step(j, carry):
        order_pair(got, j, 4, rows)
        return carry

    lax.fori_loop(0, got.shape[1] // PAIR, step, 0)

    def one(k, copy):
        real, imag = rows[k], rows[channels + k]
        left = jnp.concatenate([real, imag], axis=0)
        out[k] = gram(left, jnp.concatenate([-imag, real], axis=0))

    unrolled(channels, 8, one)


def finish_kernel(scale, got_in, prior_in, out_ref, got, prior, rows, out, sems):
    n_inp, n_chan, quads, _, _ = got.shape
    steps = n_chan // PAIR
    channels, width = out.shape[1], out.shape[-1]
    count = channels // BLOCK

    def got_copy(j):
        where = (slice(None), pl.ds(j * PAIR, PAIR))
        return pltpu.make_async_copy(got_in.at[where], got.at[where], sems.at[count + j])

    def out_copy(j):
        where = (slice(None), pl.ds(j * BLOCK, BLOCK))
        return pltpu.make_async_copy(out.at[where], out_ref.at[where], sems.at[j])

    for j in range(steps):
        got_copy(j).start()
    def prior_copy(j):
        where = pl.ds(j * BLOCK, BLOCK)
        return pltpu.make_async_copy(
            prior_in.at[where], prior.at[where], sems.at[count + steps + j]
        )

    for j in range(count):
        prior_copy(j).start()

    def order(j, carry):
        got_copy(j).wait()

        def quad(k, copy):
            for c in range(PAIR):
                times = pl.ds(pl.multiple_of((j * PAIR + c) * HALF, HALF), HALF)
                for tile in range(n_inp // 4):
                    x = lane_swap([got[tile * 4 + p, j * PAIR + c, k] for p in range(4)])
                    for p in range(4):
                        rows[4 * k + p, times, tile * LANES : (tile + 1) * LANES] = x[p]

        unrolled(quads, min(8, quads), quad)
        return carry

    lax.fori_loop(0, steps, order, 0)

    def some(j, carry):
        prior_copy(j).wait()
        for i in range(BLOCK):
            k = j * BLOCK + i
            left = rows[k]
            parts = left.astype(F32).reshape(n_chan, 2, HALF // 2, width)
            right = jnp.stack([-parts[:, 1], parts[:, 0]], axis=1).reshape(left.shape)
            value = (gram(left, right.astype(BF16)) + prior[k]) * scale
            out[0, k] = value[:, :width].astype(BF16)
            out[1, k] = value[:, width:].astype(BF16)
        out_copy(j).start()
        return carry

    lax.fori_loop(0, count, some, 0)

    def finish(j, carry):
        out_copy(j).wait()
        return carry

    lax.fori_loop(0, count, finish, 0)


def params():
    return pltpu.CompilerParams(vmem_limit_bytes=VMEM)


def cost(flops, moved):
    return pl.CostEstimate(flops=int(flops), bytes_accessed=int(moved), transcendentals=0)


def on_device(voltages, history, taper):
    in_dev, s_dev, frame = voltages.shape
    taps = taper.shape[0]
    n_inp = lax.axis_size("inp")
    n_chan = lax.axis_size("chan")
    groups = n_inp * n_chan
    channels = BAND // groups
    total = n_inp * in_dev
    times = s_dev // 2
    early = taps - 1
    blocks = LANES // in_dev
    sets = times // blocks
    span = n_chan * times
    assert frame == RADIX * LANES and in_dev == 2 * HALF and PAIR * times == HALF
    assert early == times - 1 and RADIX % channels == 0 and n_inp % blocks == 0
    assert n_chan % PAIR == 0 and channels % BLOCK == 0

    outputs = 2 * BAND // CLASSES
    stage = stage_table(frame).astype(np.float32).astype(ml_dtypes.bfloat16)
    table = jnp.asarray(stage)
    upright = jnp.asarray(np.ascontiguousarray(stage.transpose(0, 2, 1)))
    unit = jnp.asarray(np.eye(outputs).astype(ml_dtypes.bfloat16))
    assert table.shape == (CLASSES, outputs, 2 * LANES) and outputs == LANES

    away = pl.BlockSpec(memory_space=pl.ANY)
    near = pl.BlockSpec(memory_space=pltpu.VMEM)

    def scratch(count, shape):
        return [
            pltpu.VMEM(voltages.shape, BF16),
            pltpu.VMEM(taper.shape, F32),
            pltpu.VMEM(shape, BF16),
            pltpu.VMEM((RADIX, count, HALF, LANES), F32),
            pltpu.VMEM((4, 8, 8, HALF, LANES), F32),
            pltpu.VMEM((CLASSES, count * in_dev, 2 * LANES), BF16),
            pltpu.SemaphoreType.DMA((2 * CHUNKS + 2,)),
        ]

    late_shape = (sets, 2 * channels, LANES)
    early_shape = (channels // 4, HALF, LANES)

    def sent(shape):
        return jax.ShapeDtypeStruct((groups,) + shape, BF16)

    def wide(shape):
        return [
            pltpu.VMEM((RADIX, RADIX, times * in_dev), BF16),
            pltpu.VMEM((groups,) + shape, BF16),
        ]

    carried = pl.pallas_call(
        carried_kernel,
        in_specs=[away] * 3,
        out_specs=away,
        out_shape=jax.ShapeDtypeStruct((CLASSES, early * in_dev, outputs), BF16),
        scratch_shapes=scratch(early, upright.shape)
        + [
            pltpu.VMEM((CLASSES, early * in_dev, outputs), BF16),
            pltpu.SemaphoreType.DMA((CHUNKS,)),
        ],
        compiler_params=params(),
        cost_estimate=cost(1e10, 2e7),
        name="carried",
    )(voltages, taper, upright)
    carried, later_taper = lax.optimization_barrier((carried, taper))
    carried = lax.ppermute(carried, "chan", [(i, i + 1) for i in range(n_chan - 1)])

    late_send = pl.pallas_call(
        lambda *refs: spectra_kernel(times, False, *refs),
        in_specs=[away] * 3,
        out_specs=away,
        out_shape=sent(late_shape),
        scratch_shapes=scratch(times, table.shape) + wide(late_shape),
        compiler_params=params(),
        cost_estimate=cost(5e10, 4e7),
        name="late",
    )(voltages, later_taper, table)

    def exchange(value, shape):
        value = lax.all_to_all(value, ("inp", "chan"), split_axis=0, concat_axis=0, tiled=True)
        return value.reshape((n_inp, n_chan) + shape)

    late_got = exchange(late_send, late_shape)

    keep = (lax.axis_index("chan") == 0).astype(F32).reshape(1)
    early_send = pl.pallas_call(
        lambda *refs: spectra_kernel(0, True, *refs),
        in_specs=[pl.BlockSpec(memory_space=pltpu.SMEM), near, near, near] + [away] * 3,
        out_specs=away,
        out_shape=sent(early_shape),
        scratch_shapes=scratch(times, table.shape) + wide(early_shape),
        compiler_params=params(),
        cost_estimate=cost(2e11, 4e7),
        name="early",
    )(keep, jnp.transpose(history, (1, 0, 2)), carried, unit, voltages, taper, table)
    early_got = exchange(early_send, early_shape)

    rows = pltpu.VMEM((2 * channels, span, total), BF16)
    prior_shape = (channels, total, 2 * total)
    prior = pl.pallas_call(
        prior_kernel,
        in_specs=[near],
        out_specs=near,
        out_shape=jax.ShapeDtypeStruct(prior_shape, F32),
        scratch_shapes=[rows],
        compiler_params=params(),
        cost_estimate=cost(1e4, 1e4),
        name="prior",
    )(late_got)
    return pl.pallas_call(
        lambda *refs: finish_kernel(1.0 / (n_chan * s_dev), *refs),
        in_specs=[away, away],
        out_specs=away,
        out_shape=jax.ShapeDtypeStruct((2, channels, total, total), BF16),
        scratch_shapes=[
            pltpu.VMEM(early_got.shape, BF16),
            pltpu.VMEM(prior_shape, F32),
            pltpu.VMEM((channels, n_chan * HALF, total), BF16),
            pltpu.VMEM((2, channels, total, total), BF16),
            pltpu.SemaphoreType.DMA((2 * (channels // BLOCK) + n_chan // PAIR,)),
        ],
        compiler_params=params(),
        cost_estimate=cost(1e10, 1e7),
        name="finish",
    )(early_got, prior)


def solution(mesh):
    in_specs = (P("inp", "chan", None), P("inp", None, None), P())
    out_specs = P(None, ("inp", "chan"), None, None)
    return jax.shard_map(
        on_device, mesh=mesh, in_specs=in_specs, out_specs=out_specs, check_vma=False
    )
```

profile of v0, /device:TPU:0, one launch (start us, length us, event | category | flops | bytes accessed | tf_op | source)
XLA Modules:
  0.0 143.9 jit_solution(7685464871926191762)
XLA Ops:
  0.0 9.5 %carried.1 = bf16[32,224,128]{2,1,0:T(8,128)(2,1)} custom-call(bf16[32,16,8192]{2,1,0:T(8,128)(2,1)} %refs_0_.1, f32[8,8192]{1,0:T(8,128)} %refs_1_, bf16[32,256,128]{2,1,0:T(8,128)(2,1)} %constant.13.clone.table_in), custom_call_target="tpu_custom_call" | custom-call | flops 10000000000 | bytes 20000000 | tf_op jit(solution)/shard_map/carried/pallas_call | solution.py:524
  9.5 3.6 %collective-permute-start = (bf16[32,224,128]{2,1,0:T(8,128)(2,1)}, bf16[32,224,128]{2,1,0:T(8,128)(2,1)}, u32[]{:S(2)}, u32[]{:S(2)}) collective-permute-start(bf16[32,224,128]{2,1,0:T(8,128)(2,1)} %carried.1), channel_id=1, source_target_pairs={{0,1},{1,2},{2,3},{3,4},{4,5},{5,6},{6,7},{8,9},{9,10},{10,11},{11... | collective-permute-start | bytes 5505032 | tf_op jit(solution)/shard_map/ppermute | solution.py:539
  13.1 15.4 %late.1 = bf16[32,2,128,128]{3,2,1,0:T(8,128)(2,1)} custom-call(bf16[32,16,8192]{2,1,0:T(8,128)(2,1)} %refs_0_.1, f32[8,8192]{1,0:T(8,128)} %refs_1_, bf16[32,128,256]{2,1,0:T(8,128)(2,1)} %constant.12.clone.refs_6_.refs_2_), custom_call_target="tpu_custom_call" | custom-call | flops 49999998976 | bytes 40000000 | tf_op jit(solution)/shard_map/late/pallas_call | solution.py:541
  28.5 6.0 %all-to-all-start.1 = ((bf16[32,2,128,128]{3,2,1,0:T(8,128)(2,1)}), bf16[32,2,128,128]{3,2,1,0:T(8,128)(2,1)}, u32[]{:S(2)}, u32[]{:S(2)}) async-start(bf16[32,2,128,128]{3,2,1,0:T(8,128)(2,1)} %late.1), calls=%async_computation.1 | async-start | bytes 4194304 | tf_op jit(solution)/shard_map/all_to_all | solution.py:553
  34.6 0.0 collective-permute-done.refs_2_
  34.6 20.4 %early.1 = bf16[32,16,16,128]{3,2,1,0:T(8,128)(2,1)} custom-call(f32[1]{0:T(128)} %bitcast.refs_0_, bf16[7,32,8192]{2,1,0:T(8,128)(2,1)} %bitcast.4, bf16[32,224,128]{2,1,0:T(8,128)(2,1)} %collective-permute-done.refs_2_, bf16[128,128]{1,0:T(8,128)(2,1)} %constant.14.clone.refs_3_, bf16[32,16,8192]{2,1,0:T(8,128)(2,1)} %refs_0_.1, f32[8,8192]{1,0:T(8,128)} %refs_1_, ...), custom_call_target="tpu_custom_call" | custom-call | flops 199999995904 | bytes 40000000 | tf_op jit(solution)/shard_map/early/pallas_call | solution.py:559
  55.0 29.7 %all-to-all-done.1 = bf16[32,2,128,128]{3,2,1,0:T(8,128)(2,1)} async-done(((bf16[32,2,128,128]{3,2,1,0:T(8,128)(2,1)}), bf16[32,2,128,128]{3,2,1,0:T(8,128)(2,1)}, u32[]{:S(2)}, u32[]{:S(2)}) %all-to-all-start.1) | async-done | bytes 2097184 | tf_op jit(solution)/shard_map/all_to_all | solution.py:553
  84.6 3.5 %all-to-all-start = ((bf16[32,16,16,128]{3,2,1,0:T(8,128)(2,1)}), bf16[32,16,16,128]{3,2,1,0:T(8,128)(2,1)}, u32[]{:S(2)}, u32[]{:S(2)}) async-start(bf16[32,16,16,128]{3,2,1,0:T(8,128)(2,1)} %early.1), calls=%async_computation | async-start | bytes 4194304 | tf_op jit(solution)/shard_map/all_to_all | solution.py:553
  88.1 9.5 %prior.1.refs_1_ = f32[64,128,256]{2,1,0:T(8,128)} custom-call(bf16[4,8,2,128,128]{4,3,2,1,0:T(8,128)(2,1)} %bitcast.3.got), custom_call_target="tpu_custom_call" | custom-call | flops 10000 | bytes 10000 | tf_op jit(solution)/shard_map/prior/pallas_call | solution.py:573
  97.6 40.6 %all-to-all-done = bf16[32,16,16,128]{3,2,1,0:T(8,128)(2,1)} async-done(((bf16[32,16,16,128]{3,2,1,0:T(8,128)(2,1)}), bf16[32,16,16,128]{3,2,1,0:T(8,128)(2,1)}, u32[]{:S(2)}, u32[]{:S(2)}) %all-to-all-start) | async-done | bytes 2097184 | tf_op jit(solution)/shard_map/all_to_all | solution.py:553
  138.2 5.7 %finish.1 = bf16[2,64,128,128]{3,2,1,0:T(8,128)(2,1)} custom-call(bf16[4,8,16,16,128]{4,3,2,1,0:T(8,128)(2,1)} %bitcast.2.refs_0_, f32[64,128,256]{2,1,0:T(8,128)} %prior.1.refs_1_), custom_call_target="tpu_custom_call" | custom-call | flops 10000000000 | bytes 10000000 | tf_op jit(solution)/shard_map/finish/pallas_call | solution.py:583
Async XLA Ops:
  9.5 25.0 %collective-permute-start = (bf16[32,224,128]{2,1,0:T(8,128)(2,1)}, bf16[32,224,128]{2,1,0:T(8,128)(2,1)}, u32[]{:S(2)}, u32[]{:S(2)}) collective-permute-start(bf16[32,224,128]{2,1,0:T(8,128)(2,1)} %carried.1), channel_id=1, source_target_pairs={{0,1},{1,2},{2,3},{3,4},{4,5},{5,6},{6,7},{8,9},{9,10},{10,11},{11... | collective-permute-start | bytes 5505032 | tf_op jit(solution)/shard_map/ppermute | solution.py:539
  28.5 56.1 %all-to-all-start.1 = ((bf16[32,2,128,128]{3,2,1,0:T(8,128)(2,1)}), bf16[32,2,128,128]{3,2,1,0:T(8,128)(2,1)}, u32[]{:S(2)}, u32[]{:S(2)}) async-start(bf16[32,2,128,128]{3,2,1,0:T(8,128)(2,1)} %late.1), calls=%async_computation.1 | async-start | bytes 4194304 | tf_op jit(solution)/shard_map/all_to_all | solution.py:553
  84.6 53.6 %all-to-all-start = ((bf16[32,16,16,128]{3,2,1,0:T(8,128)(2,1)}), bf16[32,16,16,128]{3,2,1,0:T(8,128)(2,1)}, u32[]{:S(2)}, u32[]{:S(2)}) async-start(bf16[32,16,16,128]{3,2,1,0:T(8,128)(2,1)} %early.1), calls=%async_computation | async-start | bytes 4194304 | tf_op jit(solution)/shard_map/all_to_all | solution.py:553
where the time goes:
time: 144 us
  waiting for transfers between devices  70.3 us (49%)
  Pallas kernels  60.4 us (42%)
  starting transfers between devices  13.1 us (9%)
    all_to_all x2, waiting for transfers between devices, exchange(): lax.all_to_all(value, ('inp', 'chan'), split_axis=0, concat_axis=0, tiled...  70.3 us
    pallas_call x1, Pallas kernels, on_device(): pl.pallas_call(lambda *refs: spectra_kernel(0, True, *refs), in_specs=[pl...  20.4 us
    pallas_call x1, Pallas kernels, on_device(): pl.pallas_call(lambda *refs: spectra_kernel(times, False, *refs), in_spec...  15.4 us
    pallas_call x1, Pallas kernels, on_device(): pl.pallas_call(carried_kernel, in_specs=[away] * 3, out_specs=away, out_s...  9.54 us
    all_to_all x2, starting transfers between devices, exchange(): lax.all_to_all(value, ('inp', 'chan'), split_axis=0, concat_axis=0, tiled...  9.52 us
    pallas_call x1, Pallas kernels, on_device(): pl.pallas_call(prior_kernel, in_specs=[near], out_specs=near, out_shape=j...  9.48 us
    pallas_call x1, Pallas kernels, on_device(): pl.pallas_call(lambda *refs: finish_kernel(1.0 / (n_chan * s_dev), *refs)...  5.65 us
    ppermute x1, starting transfers between devices, on_device(): lax.ppermute(carried, 'chan', [(i, i + 1) for i in range(n_chan - 1)])  3.58 us
  transfers between devices with their start and end apart: 3, of which 2 were waited for; matrix products, arithmetic and copies ran while one was open for 0% of the time, Pallas kernels for 31%

commit v1 on v0

--- a/solution.py
+++ b/solution.py
@@ -118,9 +118,7 @@
     lax.fori_loop(0, count // copies, step, 0)
 
 
-def transform_rows(fir, mids, zed, half, copies):
-    halves = zed.shape[1] // (fir.shape[1] * HALF)
-
+def transform_rows(fir, mids, zed, copies):
     def one(s, copy):
         mid = mids.at[copy]
         for low in range(8):
@@ -131,7 +129,7 @@
                 value = turned(parts[k], low * k)
                 mid[2 * k - 1, low] = value[0]
                 mid[2 * k, low] = value[1]
-        rows = pl.ds(pl.multiple_of((s * halves + half) * HALF, HALF), HALF)
+        rows = pl.ds(pl.multiple_of(s * HALF, HALF), HALF)
 
         def put(q, half, value):
             zed[q, rows, half * LANES : (half + 1) * LANES] = value.astype(BF16)
@@ -160,7 +158,7 @@
     unrolled(fir.shape[1], copies, one)
 
 
-CHUNKS = 4
+CHUNKS = 8
 CONTRACT = (((1,), (1,)), ((), ()))
 
 
@@ -168,32 +166,31 @@
     taps = taper.shape[0]
     in_dev, s_dev, frame = volt.shape
     halves = in_dev // HALF
-    count = fir.shape[1]
+    count = fir.shape[1] // halves
     part = frame // CHUNKS
     wanted = [f for f in range(first - taps + 1, first + count) if f < s_dev]
 
-    def volt_copy(h, j):
-        where = (pl.ds(h * HALF, HALF), slice(None), pl.ds(pl.multiple_of(j * part, part), part))
-        return pltpu.make_async_copy(volt_in.at[where], volt.at[where], sems.at[h * CHUNKS + j])
-
-    taper_copy = pltpu.make_async_copy(taper_in, taper, sems.at[halves * CHUNKS])
-    table_copy = pltpu.make_async_copy(table_in, held, sems.at[halves * CHUNKS + 1])
+    def volt_copy(j):
+        where = (slice(None), slice(None), pl.ds(pl.multiple_of(j * part, part), part))
+        return pltpu.make_async_copy(volt_in.at[where], volt.at[where], sems.at[j])
+
+    taper_copy = pltpu.make_async_copy(taper_in, taper, sems.at[CHUNKS])
+    table_copy = pltpu.make_async_copy(table_in, held, sems.at[CHUNKS + 1])
     taper_copy.start()
-    for h in range(halves):
-        for j in range(CHUNKS):
-            volt_copy(h, j).start()
+    for j in range(CHUNKS):
+        volt_copy(j).start()
     table_copy.start()
     taper_copy.wait()
 
-    def one_half(h, carry):
-        inputs = pl.ds(pl.multiple_of(h * HALF, HALF), HALF)
-
-        def one_chunk(j, carry):
-            volt_copy(h, j).wait()
-
-            def one(i, copy):
-                a = j * (part // LANES) + i
-                lanes = pl.ds(pl.multiple_of(a * LANES, LANES), LANES)
+    def one_chunk(j, carry):
+        volt_copy(j).wait()
+
+        def one(i, copy):
+            a = j * (part // LANES) + i
+            lanes = pl.ds(pl.multiple_of(a * LANES, LANES), LANES)
+            weights = [taper[t : t + 1, lanes] for t in range(taps)]
+            for h in range(halves):
+                inputs = slice(h * HALF, (h + 1) * HALF)
                 by_time = jnp.swapaxes(volt[inputs, :, lanes], 0, 1)
                 frames = {}
                 for f in wanted:
@@ -201,7 +198,6 @@
                         frames[f] = by_time[f].astype(F32)
                     elif hist is not None:
                         frames[f] = hist[taps - 1 + f, inputs, lanes].astype(F32) * keep
-                weights = [taper[t : t + 1, lanes] for t in range(taps)]
                 for row in range(count):
                     total = None
                     for t in range(taps):
@@ -209,16 +205,13 @@
                         if f in frames:
                             term = weights[t] * frames[f]
                             total = term if total is None else total + term
-                    fir[a, row] = total
-
-            unrolled(part // LANES, copies[0], one)
-            return carry
-
-        lax.fori_loop(0, CHUNKS, one_chunk, 0)
-        transform_rows(fir, mid, zed, h, copies[1])
-        return carry
-
-    lax.fori_loop(0, halves, one_half, 0)
+                    fir[a, row * halves + h] = total
+
+        unrolled(part // LANES, copies[0], one)
+        return carry
+
+    lax.fori_loop(0, CHUNKS, one_chunk, 0)
+    transform_rows(fir, mid, zed, copies[1])
     table_copy.wait()
 
 
@@ -226,7 +219,7 @@
     *scratch, out, out_sems = scratch
     volt, taper, held, fir, mid, zed, sems = scratch
     fill(
-        volt.shape[1], (16, 1), None, None,
+        volt.shape[1], (4, 2), None, None,
         volt_in, taper_in, table_in, volt, taper, held, fir, mid, zed, sems,
     )
     block = CLASSES // 2
@@ -277,7 +270,7 @@
         keep, hist = None, None
     volt_in, taper_in, table_in, out_ref, volt, taper, held, fir, mid, zed, sems, wide, out = refs
     fill(
-        first, (16, 4) if boundary else (8, 2), hist, keep,
+        first, (4, 2), hist, keep,
         volt_in, taper_in, table_in, volt, taper, held, fir, mid, zed, sems,
     )
     step = RADIX
@@ -503,10 +496,10 @@
             pltpu.VMEM(voltages.shape, BF16),
             pltpu.VMEM(taper.shape, F32),
             pltpu.VMEM(shape, BF16),
-            pltpu.VMEM((RADIX, count, HALF, LANES), F32),
-            pltpu.VMEM((4, 8, 8, HALF, LANES), F32),
+            pltpu.VMEM((RADIX, 2 * count, HALF, LANES), F32),
+            pltpu.VMEM((2, 8, 8, HALF, LANES), F32),
             pltpu.VMEM((CLASSES, count * in_dev, 2 * LANES), BF16),
-            pltpu.SemaphoreType.DMA((2 * CHUNKS + 2,)),
+            pltpu.SemaphoreType.DMA((CHUNKS + 2,)),
         ]
 
     late_shape = (sets, 2 * channels, LANES)
@@ -529,7 +522,7 @@
         scratch_shapes=scratch(early, upright.shape)
         + [
             pltpu.VMEM((CLASSES, early * in_dev, outputs), BF16),
-            pltpu.SemaphoreType.DMA((CHUNKS,)),
+            pltpu.SemaphoreType.DMA((2,)),
         ],
         compiler_params=params(),
         cost_estimate=cost(1e10, 2e7),

time: 144 us -> 144 us (level)
  no operation moved by 1% of the time
where the time goes in v1:
time: 144 us
  waiting for transfers between devices  70.2 us (49%)
  Pallas kernels  60.8 us (42%)
  starting transfers between devices  13.1 us (9%)
    all_to_all x2, waiting for transfers between devices, exchange(): lax.all_to_all(value, ('inp', 'chan'), split_axis=0, concat_axis=0, tiled...  70.2 us
    pallas_call x1, Pallas kernels, on_device(): pl.pallas_call(lambda *refs: spectra_kernel(0, True, *refs), in_specs=[pl...  20.5 us
    pallas_call x1, Pallas kernels, on_device(): pl.pallas_call(lambda *refs: spectra_kernel(times, False, *refs), in_spec...  15.3 us
    pallas_call x1, Pallas kernels, on_device(): pl.pallas_call(carried_kernel, in_specs=[away] * 3, out_specs=away, out_s...  9.87 us
    all_to_all x2, starting transfers between devices, exchange(): lax.all_to_all(value, ('inp', 'chan'), split_axis=0, concat_axis=0, tiled...  9.52 us
    pallas_call x1, Pallas kernels, on_device(): pl.pallas_call(prior_kernel, in_specs=[near], out_specs=near, out_shape=j...  9.48 us
    pallas_call x1, Pallas kernels, on_device(): pl.pallas_call(lambda *refs: finish_kernel(1.0 / (n_chan * s_dev), *refs)...  5.65 us
    ppermute x1, starting transfers between devices, on_device(): lax.ppermute(carried, 'chan', [(i, i + 1) for i in range(n_chan - 1)])  3.59 us
  transfers between devices with their start and end apart: 3, of which 2 were waited for; matrix products, arithmetic and copies ran while one was open for 0% of the time, Pallas kernels for 31%

profile of v1, /device:TPU:0, one launch (start us, length us, event | category | flops | bytes accessed | tf_op | source)
XLA Modules:
  0.0 144.1 jit_solution(173626353286612379)
XLA Ops:
  0.0 9.9 %carried.1 = bf16[32,224,128]{2,1,0:T(8,128)(2,1)} custom-call(bf16[32,16,8192]{2,1,0:T(8,128)(2,1)} %refs_0_.1, f32[8,8192]{1,0:T(8,128)} %refs_1_, bf16[32,256,128]{2,1,0:T(8,128)(2,1)} %constant.13.clone.table_in), custom_call_target="tpu_custom_call" | custom-call | flops 10000000000 | bytes 20000000 | tf_op jit(solution)/shard_map/carried/pallas_call | solution.py:517
  9.9 3.6 %collective-permute-start = (bf16[32,224,128]{2,1,0:T(8,128)(2,1)}, bf16[32,224,128]{2,1,0:T(8,128)(2,1)}, u32[]{:S(2)}, u32[]{:S(2)}) collective-permute-start(bf16[32,224,128]{2,1,0:T(8,128)(2,1)} %carried.1), channel_id=1, source_target_pairs={{0,1},{1,2},{2,3},{3,4},{4,5},{5,6},{6,7},{8,9},{9,10},{10,11},{11... | collective-permute-start | bytes 5505032 | tf_op jit(solution)/shard_map/ppermute | solution.py:532
  13.5 15.3 %late.1 = bf16[32,2,128,128]{3,2,1,0:T(8,128)(2,1)} custom-call(bf16[32,16,8192]{2,1,0:T(8,128)(2,1)} %refs_0_.1, f32[8,8192]{1,0:T(8,128)} %refs_1_, bf16[32,128,256]{2,1,0:T(8,128)(2,1)} %constant.12.clone.refs_6_.refs_2_), custom_call_target="tpu_custom_call" | custom-call | flops 49999998976 | bytes 40000000 | tf_op jit(solution)/shard_map/late/pallas_call | solution.py:534
  28.8 6.0 %all-to-all-start.1 = ((bf16[32,2,128,128]{3,2,1,0:T(8,128)(2,1)}), bf16[32,2,128,128]{3,2,1,0:T(8,128)(2,1)}, u32[]{:S(2)}, u32[]{:S(2)}) async-start(bf16[32,2,128,128]{3,2,1,0:T(8,128)(2,1)} %late.1), calls=%async_computation.1 | async-start | bytes 4194304 | tf_op jit(solution)/shard_map/all_to_all | solution.py:546
  34.9 0.0 collective-permute-done.refs_2_
  34.9 20.5 %early.1 = bf16[32,16,16,128]{3,2,1,0:T(8,128)(2,1)} custom-call(f32[1]{0:T(128)} %bitcast.refs_0_, bf16[7,32,8192]{2,1,0:T(8,128)(2,1)} %bitcast.4, bf16[32,224,128]{2,1,0:T(8,128)(2,1)} %collective-permute-done.refs_2_, bf16[128,128]{1,0:T(8,128)(2,1)} %constant.14.clone.refs_3_, bf16[32,16,8192]{2,1,0:T(8,128)(2,1)} %refs_0_.1, f32[8,8192]{1,0:T(8,128)} %refs_1_, ...), custom_call_target="tpu_custom_call" | custom-call | flops 199999995904 | bytes 40000000 | tf_op jit(solution)/shard_map/early/pallas_call | solution.py:552
  55.3 29.6 %all-to-all-done.1 = bf16[32,2,128,128]{3,2,1,0:T(8,128)(2,1)} async-done(((bf16[32,2,128,128]{3,2,1,0:T(8,128)(2,1)}), bf16[32,2,128,128]{3,2,1,0:T(8,128)(2,1)}, u32[]{:S(2)}, u32[]{:S(2)}) %all-to-all-start.1) | async-done | bytes 2097184 | tf_op jit(solution)/shard_map/all_to_all | solution.py:546
  84.9 3.5 %all-to-all-start = ((bf16[32,16,16,128]{3,2,1,0:T(8,128)(2,1)}), bf16[32,16,16,128]{3,2,1,0:T(8,128)(2,1)}, u32[]{:S(2)}, u32[]{:S(2)}) async-start(bf16[32,16,16,128]{3,2,1,0:T(8,128)(2,1)} %early.1), calls=%async_computation | async-start | bytes 4194304 | tf_op jit(solution)/shard_map/all_to_all | solution.py:546
  88.4 9.5 %prior.1.refs_1_ = f32[64,128,256]{2,1,0:T(8,128)} custom-call(bf16[4,8,2,128,128]{4,3,2,1,0:T(8,128)(2,1)} %bitcast.3.got), custom_call_target="tpu_custom_call" | custom-call | flops 10000 | bytes 10000 | tf_op jit(solution)/shard_map/prior/pallas_call | solution.py:566
  97.9 40.6 %all-to-all-done = bf16[32,16,16,128]{3,2,1,0:T(8,128)(2,1)} async-done(((bf16[32,16,16,128]{3,2,1,0:T(8,128)(2,1)}), bf16[32,16,16,128]{3,2,1,0:T(8,128)(2,1)}, u32[]{:S(2)}, u32[]{:S(2)}) %all-to-all-start) | async-done | bytes 2097184 | tf_op jit(solution)/shard_map/all_to_all | solution.py:546
  138.5 5.7 %finish.1 = bf16[2,64,128,128]{3,2,1,0:T(8,128)(2,1)} custom-call(bf16[4,8,16,16,128]{4,3,2,1,0:T(8,128)(2,1)} %bitcast.2.refs_0_, f32[64,128,256]{2,1,0:T(8,128)} %prior.1.refs_1_), custom_call_target="tpu_custom_call" | custom-call | flops 10000000000 | bytes 10000000 | tf_op jit(solution)/shard_map/finish/pallas_call | solution.py:576
Async XLA Ops:
  9.9 25.0 %collective-permute-start = (bf16[32,224,128]{2,1,0:T(8,128)(2,1)}, bf16[32,224,128]{2,1,0:T(8,128)(2,1)}, u32[]{:S(2)}, u32[]{:S(2)}) collective-permute-start(bf16[32,224,128]{2,1,0:T(8,128)(2,1)} %carried.1), channel_id=1, source_target_pairs={{0,1},{1,2},{2,3},{3,4},{4,5},{5,6},{6,7},{8,9},{9,10},{10,11},{11... | collective-permute-start | bytes 5505032 | tf_op jit(solution)/shard_map/ppermute | solution.py:532
  28.8 56.1 %all-to-all-start.1 = ((bf16[32,2,128,128]{3,2,1,0:T(8,128)(2,1)}), bf16[32,2,128,128]{3,2,1,0:T(8,128)(2,1)}, u32[]{:S(2)}, u32[]{:S(2)}) async-start(bf16[32,2,128,128]{3,2,1,0:T(8,128)(2,1)} %late.1), calls=%async_computation.1 | async-start | bytes 4194304 | tf_op jit(solution)/shard_map/all_to_all | solution.py:546
  84.9 53.6 %all-to-all-start = ((bf16[32,16,16,128]{3,2,1,0:T(8,128)(2,1)}), bf16[32,16,16,128]{3,2,1,0:T(8,128)(2,1)}, u32[]{:S(2)}, u32[]{:S(2)}) async-start(bf16[32,16,16,128]{3,2,1,0:T(8,128)(2,1)} %early.1), calls=%async_computation | async-start | bytes 4194304 | tf_op jit(solution)/shard_map/all_to_all | solution.py:546

commit v2 on v1

--- a/solution.py
+++ b/solution.py
@@ -434,14 +434,22 @@
 
     lax.fori_loop(0, steps, order, 0)
 
+    row = lax.broadcasted_iota(jnp.int32, (HALF, width), 0)
+    sign = jnp.where(row < HALF // 2, -1.0, 1.0).astype(BF16)
+
     def some(j, carry):
         prior_copy(j).wait()
         for i in range(BLOCK):
             k = j * BLOCK + i
             left = rows[k]
-            parts = left.astype(F32).reshape(n_chan, 2, HALF // 2, width)
-            right = jnp.stack([-parts[:, 1], parts[:, 0]], axis=1).reshape(left.shape)
-            value = (gram(left, right.astype(BF16)) + prior[k]) * scale
+            right = jnp.concatenate(
+                [
+                    pltpu.roll(left[c * HALF : (c + 1) * HALF], HALF // 2, 0) * sign
+                    for c in range(n_chan)
+                ],
+                axis=0,
+            )
+            value = (gram(left, right) + prior[k]) * scale
             out[0, k] = value[:, :width].astype(BF16)
             out[1, k] = value[:, width:].astype(BF16)
         out_copy(j).start()

time: 144 us -> 144 us (level)
  no operation moved by 1% of the time
where the time goes in v2:
time: 144 us
  waiting for transfers between devices  70.2 us (49%)
  Pallas kernels  60.8 us (42%)
  starting transfers between devices  13.1 us (9%)
    all_to_all x2, waiting for transfers between devices, exchange(): lax.all_to_all(value, ('inp', 'chan'), split_axis=0, concat_axis=0, tiled...  70.2 us
    pallas_call x1, Pallas kernels, on_device(): pl.pallas_call(lambda *refs: spectra_kernel(0, True, *refs), in_specs=[pl...  20.5 us
    pallas_call x1, Pallas kernels, on_device(): pl.pallas_call(lambda *refs: spectra_kernel(times, False, *refs), in_spec...  15.3 us
    pallas_call x1, Pallas kernels, on_device(): pl.pallas_call(carried_kernel, in_specs=[away] * 3, out_specs=away, out_s...  9.87 us
    all_to_all x2, starting transfers between devices, exchange(): lax.all_to_all(value, ('inp', 'chan'), split_axis=0, concat_axis=0, tiled...  9.52 us
    pallas_call x1, Pallas kernels, on_device(): pl.pallas_call(prior_kernel, in_specs=[near], out_specs=near, out_shape=j...  9.48 us
    pallas_call x1, Pallas kernels, on_device(): pl.pallas_call(lambda *refs: finish_kernel(1.0 / (n_chan * s_dev), *refs)...  5.65 us
    ppermute x1, starting transfers between devices, on_device(): lax.ppermute(carried, 'chan', [(i, i + 1) for i in range(n_chan - 1)])  3.59 us
  transfers between devices with their start and end apart: 3, of which 2 were waited for; matrix products, arithmetic and copies ran while one was open for 0% of the time, Pallas kernels for 31%

profile of v2, /device:TPU:0, one launch (start us, length us, event | category | flops | bytes accessed | tf_op | source)
XLA Modules:
  0.0 144.1 jit_solution(17681656177474804823)
XLA Ops:
  0.0 9.9 %carried.1 = bf16[32,224,128]{2,1,0:T(8,128)(2,1)} custom-call(bf16[32,16,8192]{2,1,0:T(8,128)(2,1)} %refs_0_.1, f32[8,8192]{1,0:T(8,128)} %refs_1_, bf16[32,256,128]{2,1,0:T(8,128)(2,1)} %constant.13.clone.table_in), custom_call_target="tpu_custom_call" | custom-call | flops 10000000000 | bytes 20000000 | tf_op jit(solution)/shard_map/carried/pallas_call | solution.py:525
  9.9 3.6 %collective-permute-start = (bf16[32,224,128]{2,1,0:T(8,128)(2,1)}, bf16[32,224,128]{2,1,0:T(8,128)(2,1)}, u32[]{:S(2)}, u32[]{:S(2)}) collective-permute-start(bf16[32,224,128]{2,1,0:T(8,128)(2,1)} %carried.1), channel_id=1, source_target_pairs={{0,1},{1,2},{2,3},{3,4},{4,5},{5,6},{6,7},{8,9},{9,10},{10,11},{11... | collective-permute-start | bytes 5505032 | tf_op jit(solution)/shard_map/ppermute | solution.py:540
  13.5 15.3 %late.1 = bf16[32,2,128,128]{3,2,1,0:T(8,128)(2,1)} custom-call(bf16[32,16,8192]{2,1,0:T(8,128)(2,1)} %refs_0_.1, f32[8,8192]{1,0:T(8,128)} %refs_1_, bf16[32,128,256]{2,1,0:T(8,128)(2,1)} %constant.12.clone.refs_6_.refs_2_), custom_call_target="tpu_custom_call" | custom-call | flops 49999998976 | bytes 40000000 | tf_op jit(solution)/shard_map/late/pallas_call | solution.py:542
  28.8 6.0 %all-to-all-start.1 = ((bf16[32,2,128,128]{3,2,1,0:T(8,128)(2,1)}), bf16[32,2,128,128]{3,2,1,0:T(8,128)(2,1)}, u32[]{:S(2)}, u32[]{:S(2)}) async-start(bf16[32,2,128,128]{3,2,1,0:T(8,128)(2,1)} %late.1), calls=%async_computation.1 | async-start | bytes 4194304 | tf_op jit(solution)/shard_map/all_to_all | solution.py:554
  34.9 0.0 collective-permute-done.refs_2_
  34.9 20.5 %early.1 = bf16[32,16,16,128]{3,2,1,0:T(8,128)(2,1)} custom-call(f32[1]{0:T(128)} %bitcast.refs_0_, bf16[7,32,8192]{2,1,0:T(8,128)(2,1)} %bitcast.4, bf16[32,224,128]{2,1,0:T(8,128)(2,1)} %collective-permute-done.refs_2_, bf16[128,128]{1,0:T(8,128)(2,1)} %constant.14.clone.refs_3_, bf16[32,16,8192]{2,1,0:T(8,128)(2,1)} %refs_0_.1, f32[8,8192]{1,0:T(8,128)} %refs_1_, ...), custom_call_target="tpu_custom_call" | custom-call | flops 199999995904 | bytes 40000000 | tf_op jit(solution)/shard_map/early/pallas_call | solution.py:560
  55.3 29.6 %all-to-all-done.1 = bf16[32,2,128,128]{3,2,1,0:T(8,128)(2,1)} async-done(((bf16[32,2,128,128]{3,2,1,0:T(8,128)(2,1)}), bf16[32,2,128,128]{3,2,1,0:T(8,128)(2,1)}, u32[]{:S(2)}, u32[]{:S(2)}) %all-to-all-start.1) | async-done | bytes 2097184 | tf_op jit(solution)/shard_map/all_to_all | solution.py:554
  84.9 3.5 %all-to-all-start = ((bf16[32,16,16,128]{3,2,1,0:T(8,128)(2,1)}), bf16[32,16,16,128]{3,2,1,0:T(8,128)(2,1)}, u32[]{:S(2)}, u32[]{:S(2)}) async-start(bf16[32,16,16,128]{3,2,1,0:T(8,128)(2,1)} %early.1), calls=%async_computation | async-start | bytes 4194304 | tf_op jit(solution)/shard_map/all_to_all | solution.py:554
  88.4 9.5 %prior.1.refs_1_ = f32[64,128,256]{2,1,0:T(8,128)} custom-call(bf16[4,8,2,128,128]{4,3,2,1,0:T(8,128)(2,1)} %bitcast.3.got), custom_call_target="tpu_custom_call" | custom-call | flops 10000 | bytes 10000 | tf_op jit(solution)/shard_map/prior/pallas_call | solution.py:574
  97.9 40.6 %all-to-all-done = bf16[32,16,16,128]{3,2,1,0:T(8,128)(2,1)} async-done(((bf16[32,16,16,128]{3,2,1,0:T(8,128)(2,1)}), bf16[32,16,16,128]{3,2,1,0:T(8,128)(2,1)}, u32[]{:S(2)}, u32[]{:S(2)}) %all-to-all-start) | async-done | bytes 2097184 | tf_op jit(solution)/shard_map/all_to_all | solution.py:554
  138.5 5.7 %finish.1 = bf16[2,64,128,128]{3,2,1,0:T(8,128)(2,1)} custom-call(bf16[4,8,16,16,128]{4,3,2,1,0:T(8,128)(2,1)} %bitcast.2.refs_0_, f32[64,128,256]{2,1,0:T(8,128)} %prior.1.refs_1_), custom_call_target="tpu_custom_call" | custom-call | flops 10000000000 | bytes 10000000 | tf_op jit(solution)/shard_map/finish/pallas_call | solution.py:584
Async XLA Ops:
  9.9 25.0 %collective-permute-start = (bf16[32,224,128]{2,1,0:T(8,128)(2,1)}, bf16[32,224,128]{2,1,0:T(8,128)(2,1)}, u32[]{:S(2)}, u32[]{:S(2)}) collective-permute-start(bf16[32,224,128]{2,1,0:T(8,128)(2,1)} %carried.1), channel_id=1, source_target_pairs={{0,1},{1,2},{2,3},{3,4},{4,5},{5,6},{6,7},{8,9},{9,10},{10,11},{11... | collective-permute-start | bytes 5505032 | tf_op jit(solution)/shard_map/ppermute | solution.py:540
  28.8 56.1 %all-to-all-start.1 = ((bf16[32,2,128,128]{3,2,1,0:T(8,128)(2,1)}), bf16[32,2,128,128]{3,2,1,0:T(8,128)(2,1)}, u32[]{:S(2)}, u32[]{:S(2)}) async-start(bf16[32,2,128,128]{3,2,1,0:T(8,128)(2,1)} %late.1), calls=%async_computation.1 | async-start | bytes 4194304 | tf_op jit(solution)/shard_map/all_to_all | solution.py:554
  84.9 53.6 %all-to-all-start = ((bf16[32,16,16,128]{3,2,1,0:T(8,128)(2,1)}), bf16[32,16,16,128]{3,2,1,0:T(8,128)(2,1)}, u32[]{:S(2)}, u32[]{:S(2)}) async-start(bf16[32,16,16,128]{3,2,1,0:T(8,128)(2,1)} %early.1), calls=%async_computation | async-start | bytes 4194304 | tf_op jit(solution)/shard_map/all_to_all | solution.py:554

commit v3 on v1

--- a/solution.py
+++ b/solution.py
@@ -248,17 +248,19 @@
     width = LANES // 4
     block = lax.broadcasted_iota(jnp.int32, (HALF, LANES), 1) // width
     x = list(x)
-    mask = (block & 1) == 0
+    even, left, outer = (block & 1) == 0, block < 2, (block == 0) | (block == 3)
     for p in (0, 2):
         low, up = x[p], x[p + 1]
-        x[p] = jnp.where(mask, low, pltpu.roll(up, width, 1))
-        x[p + 1] = jnp.where(mask, pltpu.roll(low, LANES - width, 1), up)
-    mask = (block & 2) == 0
-    for p in (0, 1):
-        low, up = x[p], x[p + 2]
-        moved = pltpu.roll(jnp.where(mask, up, low), 2 * width, 1)
-        x[p] = jnp.where(mask, low, moved)
-        x[p + 2] = jnp.where(mask, moved, up)
+        moved = pltpu.roll(jnp.where(even, up, low), width, 1)
+        x[p] = jnp.where(even, low, moved)
+        x[p + 1] = jnp.where(even, moved, up)
+    low, up = x[0], x[2]
+    moved = pltpu.roll(jnp.where(left, up, low), 2 * width, 1)
+    x[0], x[2] = jnp.where(left, low, moved), jnp.where(left, moved, up)
+    low, up = x[1], x[3]
+    moved = pltpu.roll(jnp.where(left, up, low), 2 * width, 1)
+    stay = jnp.where(left, low, up)
+    x[1], x[3] = jnp.where(outer, moved, stay), jnp.where(outer, stay, moved)
     return x
 
 

time: 144 us -> 144 us (level)
  no operation moved by 1% of the time
where the time goes in v3:
time: 144 us
  waiting for transfers between devices  70.1 us (49%)
  Pallas kernels  60.8 us (42%)
  starting transfers between devices  13.1 us (9%)
    all_to_all x2, waiting for transfers between devices, exchange(): lax.all_to_all(value, ('inp', 'chan'), split_axis=0, concat_axis=0, tiled...  70.1 us
    pallas_call x1, Pallas kernels, on_device(): pl.pallas_call(lambda *refs: spectra_kernel(0, True, *refs), in_specs=[pl...  20.5 us
    pallas_call x1, Pallas kernels, on_device(): pl.pallas_call(lambda *refs: spectra_kernel(times, False, *refs), in_spec...  15.3 us
    pallas_call x1, Pallas kernels, on_device(): pl.pallas_call(carried_kernel, in_specs=[away] * 3, out_specs=away, out_s...  9.87 us
    pallas_call x1, Pallas kernels, on_device(): pl.pallas_call(prior_kernel, in_specs=[near], out_specs=near, out_shape=j...  9.54 us
    all_to_all x2, starting transfers between devices, exchange(): lax.all_to_all(value, ('inp', 'chan'), split_axis=0, concat_axis=0, tiled...  9.52 us
    pallas_call x1, Pallas kernels, on_device(): pl.pallas_call(lambda *refs: finish_kernel(1.0 / (n_chan * s_dev), *refs)...  5.62 us
    ppermute x1, starting transfers between devices, on_device(): lax.ppermute(carried, 'chan', [(i, i + 1) for i in range(n_chan - 1)])  3.59 us
  transfers between devices with their start and end apart: 3, of which 2 were waited for; matrix products, arithmetic and copies ran while one was open for 0% of the time, Pallas kernels for 31%

profile of v3, /device:TPU:0, one launch (start us, length us, event | category | flops | bytes accessed | tf_op | source)
XLA Modules:
  0.0 144.1 jit_solution(7068383351141103639)
XLA Ops:
  0.0 9.9 %carried.1 = bf16[32,224,128]{2,1,0:T(8,128)(2,1)} custom-call(bf16[32,16,8192]{2,1,0:T(8,128)(2,1)} %refs_0_.1, f32[8,8192]{1,0:T(8,128)} %refs_1_, bf16[32,256,128]{2,1,0:T(8,128)(2,1)} %constant.13.clone.table_in), custom_call_target="tpu_custom_call" | custom-call | flops 10000000000 | bytes 20000000 | tf_op jit(solution)/shard_map/carried/pallas_call | solution.py:519
  9.9 3.6 %collective-permute-start = (bf16[32,224,128]{2,1,0:T(8,128)(2,1)}, bf16[32,224,128]{2,1,0:T(8,128)(2,1)}, u32[]{:S(2)}, u32[]{:S(2)}) collective-permute-start(bf16[32,224,128]{2,1,0:T(8,128)(2,1)} %carried.1), channel_id=1, source_target_pairs={{0,1},{1,2},{2,3},{3,4},{4,5},{5,6},{6,7},{8,9},{9,10},{10,11},{11... | collective-permute-start | bytes 5505032 | tf_op jit(solution)/shard_map/ppermute | solution.py:534
  13.5 15.3 %late.1 = bf16[32,2,128,128]{3,2,1,0:T(8,128)(2,1)} custom-call(bf16[32,16,8192]{2,1,0:T(8,128)(2,1)} %refs_0_.1, f32[8,8192]{1,0:T(8,128)} %refs_1_, bf16[32,128,256]{2,1,0:T(8,128)(2,1)} %constant.12.clone.refs_6_.refs_2_), custom_call_target="tpu_custom_call" | custom-call | flops 49999998976 | bytes 40000000 | tf_op jit(solution)/shard_map/late/pallas_call | solution.py:536
  28.8 6.0 %all-to-all-start.1 = ((bf16[32,2,128,128]{3,2,1,0:T(8,128)(2,1)}), bf16[32,2,128,128]{3,2,1,0:T(8,128)(2,1)}, u32[]{:S(2)}, u32[]{:S(2)}) async-start(bf16[32,2,128,128]{3,2,1,0:T(8,128)(2,1)} %late.1), calls=%async_computation.1 | async-start | bytes 4194304 | tf_op jit(solution)/shard_map/all_to_all | solution.py:548
  34.9 0.0 collective-permute-done.refs_2_
  34.9 20.5 %early.1 = bf16[32,16,16,128]{3,2,1,0:T(8,128)(2,1)} custom-call(f32[1]{0:T(128)} %bitcast.refs_0_, bf16[7,32,8192]{2,1,0:T(8,128)(2,1)} %bitcast.4, bf16[32,224,128]{2,1,0:T(8,128)(2,1)} %collective-permute-done.refs_2_, bf16[128,128]{1,0:T(8,128)(2,1)} %constant.14.clone.refs_3_, bf16[32,16,8192]{2,1,0:T(8,128)(2,1)} %refs_0_.1, f32[8,8192]{1,0:T(8,128)} %refs_1_, ...), custom_call_target="tpu_custom_call" | custom-call | flops 199999995904 | bytes 40000000 | tf_op jit(solution)/shard_map/early/pallas_call | solution.py:554
  55.4 29.6 %all-to-all-done.1 = bf16[32,2,128,128]{3,2,1,0:T(8,128)(2,1)} async-done(((bf16[32,2,128,128]{3,2,1,0:T(8,128)(2,1)}), bf16[32,2,128,128]{3,2,1,0:T(8,128)(2,1)}, u32[]{:S(2)}, u32[]{:S(2)}) %all-to-all-start.1) | async-done | bytes 2097184 | tf_op jit(solution)/shard_map/all_to_all | solution.py:548
  84.9 3.5 %all-to-all-start = ((bf16[32,16,16,128]{3,2,1,0:T(8,128)(2,1)}), bf16[32,16,16,128]{3,2,1,0:T(8,128)(2,1)}, u32[]{:S(2)}, u32[]{:S(2)}) async-start(bf16[32,16,16,128]{3,2,1,0:T(8,128)(2,1)} %early.1), calls=%async_computation | async-start | bytes 4194304 | tf_op jit(solution)/shard_map/all_to_all | solution.py:548
  88.4 9.5 %prior.1.refs_1_ = f32[64,128,256]{2,1,0:T(8,128)} custom-call(bf16[4,8,2,128,128]{4,3,2,1,0:T(8,128)(2,1)} %bitcast.3.got), custom_call_target="tpu_custom_call" | custom-call | flops 10000 | bytes 10000 | tf_op jit(solution)/shard_map/prior/pallas_call | solution.py:568
  98.0 40.5 %all-to-all-done = bf16[32,16,16,128]{3,2,1,0:T(8,128)(2,1)} async-done(((bf16[32,16,16,128]{3,2,1,0:T(8,128)(2,1)}), bf16[32,16,16,128]{3,2,1,0:T(8,128)(2,1)}, u32[]{:S(2)}, u32[]{:S(2)}) %all-to-all-start) | async-done | bytes 2097184 | tf_op jit(solution)/shard_map/all_to_all | solution.py:548
  138.5 5.6 %finish.1 = bf16[2,64,128,128]{3,2,1,0:T(8,128)(2,1)} custom-call(bf16[4,8,16,16,128]{4,3,2,1,0:T(8,128)(2,1)} %bitcast.2.refs_0_, f32[64,128,256]{2,1,0:T(8,128)} %prior.1.refs_1_), custom_call_target="tpu_custom_call" | custom-call | flops 10000000000 | bytes 10000000 | tf_op jit(solution)/shard_map/finish/pallas_call | solution.py:578
Async XLA Ops:
  9.9 25.0 %collective-permute-start = (bf16[32,224,128]{2,1,0:T(8,128)(2,1)}, bf16[32,224,128]{2,1,0:T(8,128)(2,1)}, u32[]{:S(2)}, u32[]{:S(2)}) collective-permute-start(bf16[32,224,128]{2,1,0:T(8,128)(2,1)} %carried.1), channel_id=1, source_target_pairs={{0,1},{1,2},{2,3},{3,4},{4,5},{5,6},{6,7},{8,9},{9,10},{10,11},{11... | collective-permute-start | bytes 5505032 | tf_op jit(solution)/shard_map/ppermute | solution.py:534
  28.8 56.1 %all-to-all-start.1 = ((bf16[32,2,128,128]{3,2,1,0:T(8,128)(2,1)}), bf16[32,2,128,128]{3,2,1,0:T(8,128)(2,1)}, u32[]{:S(2)}, u32[]{:S(2)}) async-start(bf16[32,2,128,128]{3,2,1,0:T(8,128)(2,1)} %late.1), calls=%async_computation.1 | async-start | bytes 4194304 | tf_op jit(solution)/shard_map/all_to_all | solution.py:548
  84.9 53.6 %all-to-all-start = ((bf16[32,16,16,128]{3,2,1,0:T(8,128)(2,1)}), bf16[32,16,16,128]{3,2,1,0:T(8,128)(2,1)}, u32[]{:S(2)}, u32[]{:S(2)}) async-start(bf16[32,16,16,128]{3,2,1,0:T(8,128)(2,1)} %early.1), calls=%async_computation | async-start | bytes 4194304 | tf_op jit(solution)/shard_map/all_to_all | solution.py:548
